TPU v7x, 32 devices: a whole 2x2x4 slice. The times are simulated.
32 devices in a mesh: snap: 4 (over y, core), vtx: 8 (over z, x).
Axes of the slice: x: 2, y: 2, z: 4, core: 2. Of those that a mesh axis runs over, the one named last changes fastest.
Arguments:
- features: bfloat16 [8, 8192, 128], P('snap', 'vtx'), may hold values from -6 to 6
- tile_vals: bfloat16 [8, 64, 8, 128, 128], P('snap', 'vtx'), may hold values from -0.25 to 0.25
- tile_cols: int32 [8, 64, 8], P('snap', 'vtx'), may hold values from 0 to 63, as said below
- tile_count: int32 [8, 64], P('snap', 'vtx'), may hold values from 1 to 8
- gcn_weight: bfloat16 [128, 128], replicated, may hold values from -0.5 to 0.5
- gcn_bias: float32 [128], replicated, may hold values from -3 to 3
- input_weight: bfloat16 [128, 512], replicated, may hold values from -0.5 to 0.5
- recur_weight: bfloat16 [128, 512], replicated, may hold values from -0.5 to 0.5
- lstm_bias: float32 [512], replicated, may hold values from -4 to 4
- hidden_grad: bfloat16 [8, 1024, 8, 128], P('vtx', 'snap'), may hold values from -6 to 6
Outputs:
- hidden_states: bfloat16 [8, 1024, 8, 128], P('vtx', 'snap')
- grad_gcn_weight: float32 [128, 128], replicated
- grad_gcn_bias: float32 [128], replicated
- grad_input_weight: float32 [128, 512], replicated
- grad_recur_weight: float32 [128, 512], replicated
- grad_lstm_bias: float32 [512], replicated
Inputs may be any that keep to these rules, and one draw needn't show every extreme that they name: `tile_cols`: within one snapshot, the 8 slots of one row block name distinct column blocks, and all slots, live or not, of the row blocks j * 8 to (j + 1) * 8 - 1 together name at most one block of each group of 8 consecutive blocks.
All inputs are finite; a program needn't handle non-finite values.
Results may differ from a plain program's by a relative error of at most 0.0085.
Values may be sent and summed in bfloat16 or wider, within the bound.
A program may use at most 128 MiB of HBM per device.

v0:
```python
import jax
import jax.numpy as jnp
from jax import lax
from jax.sharding import PartitionSpec as P


def silu_slope(grad_layer, pre_act):
    squeeze = jax.nn.sigmoid(pre_act)
    return (grad_layer.astype(jnp.float32) * squeeze * (1.0 + pre_act * (1.0 - squeeze))).astype(
        jnp.bfloat16
    )


def on_device(
    features,
    tile_vals,
    tile_cols,
    tile_count,
    gcn_weight,
    gcn_bias,
    input_weight,
    recur_weight,
    lstm_bias,
    hidden_grad,
):
    steps_dev, local_verts, feat_width = features.shape
    tile_size = tile_vals.shape[3]
    hidden_size = recur_weight.shape[0]
    live_mask = lax.broadcasted_iota(jnp.int32, tile_cols.shape, 2) < tile_count[:, :, None]
    snap_iota = lax.broadcasted_iota(jnp.int32, tile_cols.shape, 0)
    gathered = lax.all_gather(features, "vtx", axis=1, tiled=True)
    whole_blocks = gathered.reshape(steps_dev, -1, tile_size, feat_width)
    fetched_blocks = whole_blocks[snap_iota, tile_cols]
    blocks_used = jnp.where(
        live_mask[..., None, None], fetched_blocks, jnp.zeros_like(fetched_blocks)
    )
    summed = jnp.einsum(
        "svmij,svmjf->svif", tile_vals, blocks_used, preferred_element_type=jnp.float32
    )
    aggregated = summed.astype(jnp.bfloat16).reshape(steps_dev * local_verts, feat_width)
    pre_act = jnp.dot(aggregated, gcn_weight, preferred_element_type=jnp.float32) + gcn_bias
    layer_out = (
        jax.nn.silu(pre_act).astype(jnp.bfloat16).reshape(steps_dev, local_verts, feat_width)
    )
    vertex_inputs = lax.all_to_all(layer_out, "snap", split_axis=1, concat_axis=0, tiled=True)
    total_steps, vertex_rows, _ = vertex_inputs.shape
    flat_inputs = vertex_inputs.reshape(total_steps * vertex_rows, feat_width)
    input_gates = (
        jnp.dot(flat_inputs, input_weight, preferred_element_type=jnp.float32) + lstm_bias
    ).reshape(total_steps, vertex_rows, 4 * hidden_size)

    def advance(carried, gates_step):
        cell_state, last_out = carried
        pre_gates = gates_step + jnp.dot(last_out, recur_weight, preferred_element_type=jnp.float32)
        gate_in = jax.nn.sigmoid(pre_gates[:, :hidden_size])
        gate_keep = jax.nn.sigmoid(pre_gates[:, hidden_size : 2 * hidden_size])
        gate_new = jnp.tanh(pre_gates[:, 2 * hidden_size : 3 * hidden_size])
        gate_out = jax.nn.sigmoid(pre_gates[:, 3 * hidden_size :])
        cell_state = gate_keep * cell_state + gate_in * gate_new
        new_out = (gate_out * jnp.tanh(cell_state)).astype(jnp.bfloat16)
        return ((cell_state, new_out), (pre_gates, cell_state, new_out))

    zero_cell = jnp.zeros((vertex_rows, hidden_size), jnp.float32)
    start = (zero_cell, jnp.zeros((vertex_rows, hidden_size), jnp.bfloat16))
    _, (all_pre, all_cells, all_outs) = lax.scan(advance, start, input_gates)
    prev_cells = jnp.concatenate([zero_cell[None], all_cells[:-1]], axis=0)
    prev_outs = jnp.concatenate([start[1][None], all_outs[:-1]], axis=0)
    grad_outs = jnp.transpose(hidden_grad[0], (1, 0, 2)).astype(jnp.float32)

    def retreat(carried, step_items):
        grad_cell, grad_back = carried
        pre_gates, cell_state, prev_cell, grad_out = step_items
        gate_in = jax.nn.sigmoid(pre_gates[:, :hidden_size])
        gate_keep = jax.nn.sigmoid(pre_gates[:, hidden_size : 2 * hidden_size])
        gate_new = jnp.tanh(pre_gates[:, 2 * hidden_size : 3 * hidden_size])
        gate_out = jax.nn.sigmoid(pre_gates[:, 3 * hidden_size :])
        squash = jnp.tanh(cell_state)
        grad_total = grad_out + grad_back
        grad_cell = grad_cell + grad_total * gate_out * (1.0 - squash * squash)
        grad_gates = jnp.concatenate(
            [
                grad_cell * gate_new * gate_in * (1.0 - gate_in),
                grad_cell * prev_cell * gate_keep * (1.0 - gate_keep),
                grad_cell * gate_in * (1.0 - gate_new * gate_new),
                grad_total * squash * gate_out * (1.0 - gate_out),
            ],
            axis=1,
        ).astype(jnp.bfloat16)
        grad_back = jnp.einsum(
            "rg,hg->rh", grad_gates, recur_weight, preferred_element_type=jnp.float32
        )
        return ((grad_cell * gate_keep, grad_back), grad_gates)

    _, all_grad_gates = lax.scan(
        retreat, (zero_cell, zero_cell), (all_pre, all_cells, prev_cells, grad_outs), reverse=True
    )
    flat_gates = all_grad_gates.reshape(total_steps * vertex_rows, 4 * hidden_size)
    grad_input = jnp.einsum(
        "rf,rg->fg", flat_inputs, flat_gates, preferred_element_type=jnp.float32
    )
    grad_recur = jnp.einsum(
        "rh,rg->hg",
        prev_outs.reshape(total_steps * vertex_rows, hidden_size),
        flat_gates,
        preferred_element_type=jnp.float32,
    )
    grad_bias = jnp.sum(flat_gates.astype(jnp.float32), axis=0)
    grad_layer = jnp.einsum(
        "rg,fg->rf", flat_gates, input_weight, preferred_element_type=jnp.float32
    ).astype(jnp.bfloat16)
    grad_snap = lax.all_to_all(
        grad_layer.reshape(total_steps, vertex_rows, feat_width),
        "snap",
        split_axis=0,
        concat_axis=1,
        tiled=True,
    )
    grad_snap = grad_snap.reshape(steps_dev * local_verts, feat_width)
    grad_pre = silu_slope(grad_snap, pre_act)
    grad_gcn = jnp.einsum("rf,rg->fg", aggregated, grad_pre, preferred_element_type=jnp.float32)
    grad_gbias = jnp.sum(grad_pre.astype(jnp.float32), axis=0)
    grad_gcn, grad_gbias, grad_input, grad_recur, grad_bias = lax.psum(
        (grad_gcn, grad_gbias, grad_input, grad_recur, grad_bias), ("snap", "vtx")
    )
    hidden_states = jnp.transpose(all_outs, (1, 0, 2))[None]
    return (hidden_states, grad_gcn, grad_gbias, grad_input, grad_recur, grad_bias)


def solution(mesh):
    return jax.shard_map(
        on_device,
        mesh=mesh,
        in_specs=(
            P("snap", "vtx", None),
            P("snap", "vtx", None, None, None),
            P("snap", "vtx", None),
            P("snap", "vtx"),
            P(),
            P(),
            P(),
            P(),
            P(),
            P("vtx", "snap", None, None),
        ),
        out_specs=(P("vtx", "snap", None, None), P(), P(), P(), P(), P()),
        check_vma=False,
    )
```

profile of v0, /device:TPU:0, one launch (start us, length us, event | category | flops | bytes accessed | tf_op | source)
XLA Modules:
  0.0 330.1 jit_solution(17149991569999651273)
XLA Ops:
  9.5 76.8 %all-gather.2.cloned.1.call-done = bf16[2,8192,128]{2,1,0:T(8,128)(2,1)} async-done(((bf16[2,1024,128]{2,1,0:T(8,128)(2,1)}), bf16[2,8192,128]{2,1,0:T(8,128)(2,1)}) %all-gather.2.cloned.1.call-update) | async-done | bytes 4194320 | tf_op jit(solution)/shard_map/all_gather | solution.py:31
  86.3 5.3 %gather_fusion = bf16[128,128,128]{2,1,0:T(8,128)(2,1)} fusion(bf16[2,64,128,128]{3,2,1,0:T(8,128)(2,1)} %bitcast.139, s32[128]{0:T(128)S(1)} %reshape.144), kind=kCustom, calls=%fused_computation | custom fusion | bytes 8389632 | tf_op jit(solution)/shard_map/gather | solution.py:33
  91.6 4.8 %fusion.53 = bf16[2,8,128,128]{2,3,1,0:T(8,128)(2,1)S(1)} fusion(bf16[2,8,8,128,128]{4,3,2,1,0:T(8,128)(2,1)} %param.15, bf16[2,8,8,128,128]{4,3,2,1,0:T(8,128)(2,1)} %bitcast.140, pred[2,8,8]{2,1,0:T(8,128)(4,1)S(1)} %iota_compare_fusion), kind=kOutput, calls=%fused_computation.77 | convolution fusion | flops 539230208 | bytes 8913024 | tf_op jit(solution)/shard_map/svmij,svmjf->svif/dot_general | solution.py:37
  100.0 3.5 %all-to-all-start = ((bf16[2,1024,128]{2,0,1:T(2,128)(2,1)}), bf16[2,1024,128]{2,0,1:T(2,128)(2,1)S(1)}, u32[]{:S(2)}, u32[]{:S(2)}) async-start(bf16[2,1024,128]{2,0,1:T(2,128)(2,1)} %copy.28), calls=%async_computation | async-start | bytes 1048576 | tf_op jit(solution)/shard_map/all_to_all | solution.py:45
  104.6 7.7 %all-to-all-done = bf16[2,1024,128]{2,0,1:T(2,128)(2,1)S(1)} async-done(((bf16[2,1024,128]{2,0,1:T(2,128)(2,1)}), bf16[2,1024,128]{2,0,1:T(2,128)(2,1)S(1)}, u32[]{:S(2)}, u32[]{:S(2)}) %all-to-all-start) | async-done | bytes 524320 | tf_op jit(solution)/shard_map/all_to_all | solution.py:45
  112.4 2.6 convolution_add_fusion.1
  115.0 23.1 %while.38 = (s32[]{:T(128)}, f32[256,128]{1,0:T(8,128)S(1)}, bf16[256,128]{1,0:T(8,128)(2,1)S(1)}, f32[8,256,512]{2,1,0:T(8,128)}, f32[8,256,128]{2,1,0:T(8,128)...) while((s32[]{:T(128)}, f32[256,128]{1,0:T(8,128)S(1)}, ...), condition=%wide.region_1.2_spmd.clone, body=%wide.region_0.1_spmd.clone.sunk | while | flops 34209792 | bytes 2950260 | solution.py:65
  115.0 2.1 bitcast_dynamic-update-slice_fusion.6
  117.9 2.1 bitcast_dynamic-update-slice_fusion.6
  120.8 2.1 bitcast_dynamic-update-slice_fusion.6
  123.7 2.1 bitcast_dynamic-update-slice_fusion.6
  126.5 2.0 bitcast_dynamic-update-slice_fusion.6
  129.4 2.1 bitcast_dynamic-update-slice_fusion.6
  132.3 2.1 bitcast_dynamic-update-slice_fusion.6
  135.2 2.1 bitcast_dynamic-update-slice_fusion.6
  139.6 33.9 %while.39 = (s32[]{:T(128)}, f32[256,128]{1,0:T(8,128)}, f32[256,128]{1,0:T(8,128)S(1)}, bf16[8,256,512]{2,1,0:T(8,128)(2,1)S(1)}, f32[8,256,128]{2,1,0:T(8,128)...) while((s32[]{:T(128)}, f32[256,128]{1,0:T(8,128)}, ...), condition=%wide.region_3.4_spmd.clone, body=%wide.region_2.3_spmd.clone.sunk | while | flops 36962308 | bytes 4194459 | solution.py:94
  141.9 1.7 fusion.92
  167.3 1.7 fusion.92
  173.5 2.1 copy.34
  177.1 3.5 %all-to-all-start.1 = ((bf16[8,256,128]{2,1,0:T(8,128)(2,1)}), bf16[8,256,128]{2,1,0:T(8,128)(2,1)S(1)}, u32[]{:S(2)}, u32[]{:S(2)}) async-start(bf16[8,256,128]{2,1,0:T(8,128)(2,1)} %bitcast.143), calls=%async_computation.1 | async-start | bytes 1048576 | tf_op jit(solution)/shard_map/all_to_all | solution.py:111
  180.6 2.2 convolution_bitcast_fusion
  184.0 5.4 %all-to-all-done.1 = bf16[8,256,128]{2,1,0:T(8,128)(2,1)S(1)} async-done(((bf16[8,256,128]{2,1,0:T(8,128)(2,1)}), bf16[8,256,128]{2,1,0:T(8,128)(2,1)S(1)}, u32[]{:S(2)}, u32[]{:S(2)}) %all-to-all-start.1) | async-done | bytes 524320 | tf_op jit(solution)/shard_map/all_to_all | solution.py:111
  193.6 38.7 %all-reduce.2 = (f32[128]{0:T(128)}, f32[512]{0:T(512)}) all-reduce(f32[128]{0:T(128)S(1)} %get-tuple-element.334, f32[512]{0:T(512)S(1)} %convert_reduce_fusion), channel_id=1, replica_groups=mesh['snap'=4,'vtx'=8] {'snap','vtx'}, use_global_device_ids=true, to_apply=%region_6.7 | all-reduce | flops 640 | bytes 5120 | tf_op jit(solution)/shard_map/psum | solution.py:122
  232.2 86.2 %all-reduce.6.cloned.1.call-done = (f32[128,128]{1,0:T(8,128)}, f32[128,512]{1,0:T(8,128)}, f32[128,512]{1,0:T(8,128)}) async-done(((f32[128,128]{1,0:T(8,128)}, f32[128,512]{1,0:T(8,128)}, f32[128,512]{1,0:T(8,128)}), (f32[128,128]{1,0:T(8,128)}, f32[128,512]{1,0:T(8,128)}, f32[128,512]{1,0:T(8,128)})) %all-reduce.6.cloned.1.call-update) | async-done | bytes 589840 | tf_op jit(solution)/shard_map/psum | solution.py:122
  (109 shorter events, 56.8 us)
Async XLA Ops:
  7.2 105.2 %copy-start = (bf16[128,512]{1,0:T(8,128)(2,1)S(1)}, bf16[128,512]{1,0:T(8,128)(2,1)}, u32[]{:S(2)}) copy-start(bf16[128,512]{1,0:T(8,128)(2,1)} %param.20) | copy-start | bytes 393220
  7.2 79.1 %all-gather.2.cloned.1.call-start = ((), (), s32[]{:S(2)}) async-start(), calls=%async_computation.2 | async-start | bytes 4718592 | tf_op jit(solution)/shard_map/all_gather | solution.py:31
  91.6 5.6 %copy-start.9 = (bf16[128,128]{1,0:T(8,128)(2,1)S(1)}, bf16[128,128]{1,0:T(8,128)(2,1)}, u32[]{:S(2)}) copy-start(bf16[128,128]{1,0:T(8,128)(2,1)} %param.18) | copy-start | bytes 98308
  91.6 5.6 %copy-start.10 = (f32[128]{0:T(128)S(1)}, f32[128]{0:T(128)}, u32[]{:S(2)}) copy-start(f32[128]{0:T(128)} %param.19) | copy-start | bytes 1540
  96.4 0.8 copy-start.6
  96.4 7.1 %copy-start.5 = (bf16[1,256,8,128]{3,2,1,0:T(8,128)(2,1)S(1)}, bf16[1,256,8,128]{3,2,1,0:T(8,128)(2,1)}, u32[]{:S(2)}) copy-start(bf16[1,256,8,128]{3,2,1,0:T(8,128)(2,1)} %param.23) | copy-start | bytes 1572868
  98.6 13.8 %copy-start.8 = (f32[512]{0:T(512)S(1)}, f32[512]{0:T(512)}, u32[]{:S(2)}) copy-start(f32[512]{0:T(512)} %param.22) | copy-start | bytes 6148
  100.0 12.3 %all-to-all-start = ((bf16[2,1024,128]{2,0,1:T(2,128)(2,1)}), bf16[2,1024,128]{2,0,1:T(2,128)(2,1)S(1)}, u32[]{:S(2)}, u32[]{:S(2)}) async-start(bf16[2,1024,128]{2,0,1:T(2,128)(2,1)} %copy.28), calls=%async_computation | async-start | bytes 1048576 | tf_op jit(solution)/shard_map/all_to_all | solution.py:45
  103.5 11.5 %copy-start.1 = (bf16[128,512]{1,0:T(8,128)(2,1)S(1)}, bf16[128,512]{1,0:T(8,128)(2,1)}, u32[]{:S(2)}) copy-start(bf16[128,512]{1,0:T(8,128)(2,1)} %param.21) | copy-start | bytes 393220
  138.1 1.3 copy-start.2
  177.1 12.3 %all-to-all-start.1 = ((bf16[8,256,128]{2,1,0:T(8,128)(2,1)}), bf16[8,256,128]{2,1,0:T(8,128)(2,1)S(1)}, u32[]{:S(2)}, u32[]{:S(2)}) async-start(bf16[8,256,128]{2,1,0:T(8,128)(2,1)} %bitcast.143), calls=%async_computation.1 | async-start | bytes 1048576 | tf_op jit(solution)/shard_map/all_to_all | solution.py:111
  180.6 137.8 %all-reduce.6.cloned.1.call-start = ((), (), s32[]{:S(2)}) async-start(), calls=%async_computation.3 | async-start | bytes 1179648 | tf_op jit(solution)/shard_map/psum | solution.py:122
  184.0 8.1 %copy-start.3 = (bf16[8,256,128]{2,1,0:T(8,128)(2,1)S(1)}, bf16[8,256,128]{2,1,0:T(8,128)(2,1)}, u32[]{:S(2)}) copy-start(bf16[8,256,128]{2,1,0:T(8,128)(2,1)} %get-tuple-element.229) | copy-start | bytes 1572868
  189.4 1.2 copy-start.4
  189.4 1.7 copy-start.7
Sparse Core Ops, SparseCore 0:
  10.2 76.0 all-gather.1
  192.2 126.1 all-reduce.5
where the time goes:
time: 332 us; the launch traced here: 330 us
  waiting for transfers between devices  177 us (53%)
  blocking collectives  38.7 us (12%)
  matrix products  33 us (10%)
  other arithmetic  32.8 us (10%)
  local copies, waits for them, and re-layouts  27 us (8%)
  between operations  14.3 us (4%)
  starting transfers between devices  7.02 us (2%)
    psum x1, waiting for transfers between devices, on_device(): lax.psum((grad_gcn, grad_gbias, grad_input, grad_recur, grad_bias), ('sna...  86.2 us
    all_gather x1, waiting for transfers between devices, on_device(): gathered = lax.all_gather(features, 'vtx', axis=1, tiled=True)  76.8 us
    psum x1, blocking collectives, on_device(): lax.psum((grad_gcn, grad_gbias, grad_input, grad_recur, grad_bias), ('sna...  38.7 us
    another operation x16, other arithmetic  22.8 us
    dot_general x8, matrix products, advance(): jnp.dot(last_out, recur_weight, preferred_element_type=jnp.float32)  16.5 us
    squeeze x8, local copies, waits for them, and re-layouts, on_device(): _, (all_pre, all_cells, all_outs) = lax.scan(advance, start, input_gates)  8.64 us
    all_to_all x1, waiting for transfers between devices, on_device(): lax.all_to_all(layer_out, 'snap', split_axis=1, concat_axis=0, tiled=True)  7.67 us
    unnamed x25, local copies, waits for them, and re-layouts  6.77 us
  transfers between devices with their start and end apart: 4, of which 4 were waited for; matrix products, arithmetic and copies ran while one was open for 2% of the time, Pallas kernels for 0%

commit v1 on v0

v1 whole, which is shorter than its diff:
```python
import functools

import jax
import jax.numpy as jnp
from jax import lax
from jax.experimental import pallas as pl
from jax.experimental.pallas import tpu as pltpu
from jax.sharding import PartitionSpec as P

MESH = pl.DeviceIdType.MESH
LANES = 128


def sigmoid(x):
    return 0.5 * jnp.tanh(0.5 * x) + 0.5


class Reducer:
    def __init__(self, me, sizes, own, part_in, part_sum, chunk_in, whole, sems):
        self.me, self.sizes = me, sizes
        self.own, self.part_in, self.part_sum = own, part_in, part_sum
        self.chunk_in, self.whole, self.sems = chunk_in, whole, sems
        self.part = part_sum.shape[0]
        self.chunk = self.part // sizes["vtx"]

    def rows(self, snap, vtx=None):
        if vtx is None:
            return pl.ds(pl.multiple_of(snap * self.part, self.part), self.part)
        return pl.ds(pl.multiple_of(snap * self.part + vtx * self.chunk, self.chunk), self.chunk)

    def copy(self, stage, k, forward):
        axis = ("snap", "vtx", "vtx", "snap")[stage]
        n, me = self.sizes[axis], self.me[axis]
        peer = lax.rem(me + k, n) if forward else lax.rem(me - k + n, n)
        if stage == 0:
            src, dst = self.own.at[self.rows(peer)], self.part_in.at[k - 1]
        elif stage == 1:
            here = pl.ds(pl.multiple_of(peer * self.chunk, self.chunk), self.chunk)
            src, dst = self.part_sum.at[here], self.chunk_in.at[k - 1]
        elif stage == 2:
            src = dst = self.whole.at[self.rows(self.me["snap"], me if forward else peer)]
        else:
            src = dst = self.whole.at[self.rows(me if forward else peer)]
        return pltpu.make_async_remote_copy(
            src_ref=src,
            dst_ref=dst,
            send_sem=self.sems.at[2 * stage, k],
            recv_sem=self.sems.at[2 * stage + 1, k],
            device_id={axis: peer},
            device_id_type=MESH,
        )

    def peers(self, stage):
        return range(1, self.sizes[("snap", "vtx", "vtx", "snap")[stage]])

    def start(self, stage):
        for k in self.peers(stage):
            self.copy(stage, k, True).start()

    def finish(self, stage):
        for k in self.peers(stage):
            self.copy(stage, k, False).wait_recv()
        if stage == 0:
            total = self.own[self.rows(self.me["snap"]), :]
            for k in self.peers(stage):
                total = total + self.part_in[k - 1].astype(jnp.float32)
            self.part_sum[...] = total
        elif stage == 1:
            here = pl.ds(pl.multiple_of(self.me["vtx"] * self.chunk, self.chunk), self.chunk)
            total = self.part_sum[here, :]
            for k in self.peers(stage):
                total = total + self.chunk_in[k - 1].astype(jnp.float32)
            place = self.rows(self.me["snap"], self.me["vtx"])
            self.whole[place, :] = total.astype(self.whole.dtype)

    def drain(self):
        for stage in range(4):
            for k in self.peers(stage):
                self.copy(stage, k, True).wait_send()


def kernel(
    sizes,
    request_ref,
    place_ref,
    feat_ref,
    tiles_ref,
    gcn_w_ref,
    gcn_b_ref,
    in_w_ref,
    rec_w_ref,
    lstm_b_ref,
    hgrad_ref,
    hid_out,
    gcn_out,
    gcn_b_out,
    in_out,
    rec_out,
    lstm_b_out,
    tiles,
    asked,
    staged,
    fetched,
    aggregated,
    pre_act,
    layer,
    xs,
    hs,
    acts,
    cells,
    dlayer,
    dlayer_in,
    dcell,
    back,
    weights,
    weights_t,
    lstm_b_sum,
    sum1,
    part_in1,
    part1,
    chunk_in1,
    whole1,
    sum2,
    part_in2,
    part2,
    chunk_in2,
    whole2,
    tile_sem,
    ask_sem,
    feat_sem,
    layer_sem,
    back_send,
    back_recv,
    sems1,
    sems2,
):
    ns, nv = sizes["snap"], sizes["vtx"]
    me_s, me_v = lax.axis_index("snap"), lax.axis_index("vtx")
    me = {"snap": me_s, "vtx": me_v}
    steps, verts, width = layer.shape
    _, row_blocks, slots, tile, _ = tiles_ref.shape
    total_steps, rows, hid = hgrad_ref.shape

    def remote(src, dst, send, recv, axis, peer):
        return pltpu.make_async_remote_copy(
            src_ref=src,
            dst_ref=dst,
            send_sem=send,
            recv_sem=recv,
            device_id={axis: peer},
            device_id_type=MESH,
        )

    barrier = pltpu.get_barrier_semaphore()
    for axis in ("snap", "vtx"):
        for k in range(1, sizes[axis]):
            peer = lax.rem(me[axis] + k, sizes[axis])
            pl.semaphore_signal(barrier, inc=1, device_id={axis: peer}, device_id_type=MESH)
    load_tiles = pltpu.make_async_copy(tiles_ref, tiles, tile_sem)
    load_tiles.start()
    fetched[nv] = jnp.zeros((steps, tile, width), jnp.bfloat16)
    weights[...] = jnp.concatenate([in_w_ref[...], rec_w_ref[...]], axis=0)
    weights_t[...] = weights[...].T
    pl.semaphore_wait(barrier, ns + nv - 2)

    def ask(k, forward):
        peer = lax.rem(me_v + k, nv) if forward else lax.rem(me_v - k + nv, nv)
        return remote(
            request_ref.at[peer], asked.at[k], ask_sem.at[0, k], ask_sem.at[1, k], "vtx", peer
        )

    def give(k, forward):
        peer = lax.rem(me_v + k, nv) if forward else lax.rem(me_v - k + nv, nv)
        return remote(
            staged.at[k],
            fetched.at[me_v if forward else peer],
            feat_sem.at[0, k],
            feat_sem.at[1, k],
            "vtx",
            peer,
        )

    for k in range(1, nv):
        ask(k, True).start()
    own_request = request_ref[me_v]
    for s in range(steps):
        fetched[me_v, s] = feat_ref[s, own_request[s, 0]]
    for k in range(1, nv):
        ask(nv - k, False).wait_recv()
        wanted = asked[nv - k]
        for s in range(steps):
            staged[k, s] = feat_ref[s, wanted[s, 0]]
        give(k, True).start()
    for k in range(1, nv):
        give(k, False).wait_recv()
    load_tiles.wait()

    def layer_copy(k, s, forward):
        peer = lax.rem(me_s + k, ns) if forward else lax.rem(me_s - k + ns, ns)
        holder = me_s if forward else peer
        return remote(
            layer.at[s, pl.ds(pl.multiple_of(peer * rows, rows), rows)],
            xs.at[holder * steps + s],
            layer_sem.at[0, k, s],
            layer_sem.at[1, k, s],
            "snap",
            peer,
        )

    def convolve(s, carry):
        for r in range(row_blocks):
            picked = [fetched[place_ref[s, r, m], s] for m in range(slots)]
            left = jnp.concatenate([tiles[s, r, m] for m in range(slots)], axis=1)
            summed = jnp.dot(
                left, jnp.concatenate(picked, axis=0), preferred_element_type=jnp.float32
            )
            aggregated[s, pl.ds(r * tile, tile), :] = summed.astype(jnp.bfloat16)
        pre = (
            jnp.dot(aggregated[s], gcn_w_ref[...], preferred_element_type=jnp.float32)
            + gcn_b_ref[...]
        )
        pre_act[s] = pre
        layer[s] = (pre * sigmoid(pre)).astype(jnp.bfloat16)
        for k in range(1, ns):
            layer_copy(k, s, True).start()
        xs[me_s * steps + s] = layer[s, pl.ds(pl.multiple_of(me_s * rows, rows), rows), :]
        return carry

    lax.fori_loop(0, steps, convolve, 0)

    hs[0] = jnp.zeros((rows, hid), jnp.bfloat16)
    cells[0] = jnp.zeros((rows, hid), jnp.float32)

    def advance(t, carry):
        holder = lax.div(t, steps)

        @pl.when(holder != me_s)
        def _():
            k = lax.rem(me_s - holder + ns, ns)
            layer_copy(k, lax.rem(t, steps), False).wait_recv()

        both = jnp.concatenate([xs[t], hs[t]], axis=1)
        gates = jnp.dot(both, weights[...], preferred_element_type=jnp.float32) + lstm_b_ref[...]
        gate_in = sigmoid(gates[:, :hid])
        gate_keep = sigmoid(gates[:, hid : 2 * hid])
        gate_new = jnp.tanh(gates[:, 2 * hid : 3 * hid])
        gate_out = sigmoid(gates[:, 3 * hid :])
        cell = gate_keep * cells[t] + gate_in * gate_new
        out = (gate_out * jnp.tanh(cell)).astype(jnp.bfloat16)
        acts[t, 0] = gate_in
        acts[t, 1] = gate_keep
        acts[t, 2] = gate_new
        acts[t, 3] = gate_out
        cells[t + 1] = cell
        hs[t + 1] = out
        hid_out[t] = out
        return carry

    lax.fori_loop(0, total_steps, advance, 0)

    def back_copy(t, peer, forward):
        holder = lax.div(t, steps)
        s = lax.rem(t, steps)
        k = lax.rem(holder - me_s + ns, ns) if forward else lax.rem(me_s - peer + ns, ns)
        sender = me_s if forward else peer
        return remote(
            dlayer.at[t],
            dlayer_in.at[s, pl.ds(pl.multiple_of(sender * rows, rows), rows)],
            back_send.at[t],
            back_recv.at[k, s],
            "snap",
            holder if forward else peer,
        )

    dcell[...] = jnp.zeros((rows, hid), jnp.float32)
    back[...] = jnp.zeros((rows, hid), jnp.float32)
    lstm_b_sum[...] = jnp.zeros(lstm_b_sum.shape, jnp.float32)
    sum1[...] = jnp.zeros(sum1.shape, jnp.float32)
    height = width + hid

    def retreat(step, carry):
        t = total_steps - 1 - step
        gate_in, gate_keep, gate_new, gate_out = (acts[t, q] for q in range(4))
        squash = jnp.tanh(cells[t + 1])
        dh = hgrad_ref[t].astype(jnp.float32) + back[...]
        dc = dcell[...] + dh * gate_out * (1.0 - squash * squash)
        dgates = jnp.concatenate(
            [
                dc * gate_new * gate_in * (1.0 - gate_in),
                dc * cells[t] * gate_keep * (1.0 - gate_keep),
                dc * gate_in * (1.0 - gate_new * gate_new),
                dh * squash * gate_out * (1.0 - gate_out),
            ],
            axis=1,
        ).astype(jnp.bfloat16)
        dcell[...] = dc * gate_keep
        both_back = jnp.dot(dgates, weights_t[...], preferred_element_type=jnp.float32)
        back[...] = both_back[:, width:]
        grad = both_back[:, :width].astype(jnp.bfloat16)
        holder = lax.div(t, steps)

        @pl.when(holder != me_s)
        def _():
            dlayer[t] = grad
            back_copy(t, None, True).start()

        @pl.when(holder == me_s)
        def _():
            place = pl.ds(pl.multiple_of(me_s * rows, rows), rows)
            dlayer_in[lax.rem(t, steps), place, :] = grad

        lstm_b_sum[...] += jnp.sum(
            dgates.astype(jnp.float32).reshape(rows // 8, 8, 4 * hid), axis=0
        )
        both = jnp.concatenate([xs[t], hs[t]], axis=1)
        term = lax.dot_general(
            both, dgates, (((0,), (0,)), ((), ())), preferred_element_type=jnp.float32
        )
        for q in range(4):
            sum1[q * height : (q + 1) * height, :] += term[:, q * hid : (q + 1) * hid]
        return carry

    lax.fori_loop(0, total_steps, retreat, 0)

    first = Reducer(me, sizes, sum1, part_in1, part1, chunk_in1, whole1, sems1)
    second = Reducer(me, sizes, sum2, part_in2, part2, chunk_in2, whole2, sems2)
    first.start(0)

    sum2[...] = jnp.zeros(sum2.shape, jnp.float32)
    gcn_b_sum = jnp.zeros((1, width), jnp.float32)
    for s in reversed(range(steps)):
        for k in range(1, ns):
            src = lax.rem(me_s - k + ns, ns)
            back_copy(me_s * steps + s, src, False).wait_recv()
        pre = pre_act[s]
        slope = sigmoid(pre)
        dpre = (dlayer_in[s].astype(jnp.float32) * slope * (1.0 + pre * (1.0 - slope))).astype(
            jnp.bfloat16
        )
        sum2[:width, :] += lax.dot_general(
            aggregated[s], dpre, (((0,), (0,)), ((), ())), preferred_element_type=jnp.float32
        )
        gcn_b_sum = gcn_b_sum + jnp.sum(dpre.astype(jnp.float32), axis=0, keepdims=True)
    lstm_b = jnp.sum(lstm_b_sum[...], axis=0, keepdims=True)
    sum2[width : width + 1, :] = gcn_b_sum
    for q in range(4):
        sum2[width + 1 + q : width + 2 + q, :] = lstm_b[:, q * hid : (q + 1) * hid]

    second.start(0)
    for stage in range(4):
        first.finish(stage)
        if stage < 3:
            first.start(stage + 1)
        second.finish(stage)
        if stage < 3:
            second.start(stage + 1)

    for q in range(4):
        at = q * height
        span = slice(q * hid, (q + 1) * hid)
        in_out[:, span] = whole1[at : at + width, :].astype(jnp.float32)
        rec_out[:, span] = whole1[at + width : at + height, :].astype(jnp.float32)
        lstm_b_out[:, span] = whole2[width + 1 + q : width + 2 + q, :]
    gcn_out[...] = whole2[:width, :]
    gcn_b_out[...] = whole2[width : width + 1, :]

    for k in range(1, nv):
        ask(k, True).wait_send()
        give(k, True).wait_send()
    for k in range(1, ns):
        for s in range(steps):
            layer_copy(k, s, True).wait_send()

    def drain(t, carry):
        @pl.when(lax.div(t, steps) != me_s)
        def _():
            back_copy(t, None, True).wait_send()

        return carry

    lax.fori_loop(0, total_steps, drain, 0)
    first.drain()
    second.drain()


def on_device(
    sizes,
    features,
    tile_vals,
    tile_cols,
    tile_count,
    gcn_weight,
    gcn_bias,
    input_weight,
    recur_weight,
    lstm_bias,
    hidden_grad,
):
    ns, nv = sizes["snap"], sizes["vtx"]
    steps, verts, width = features.shape
    _, row_blocks, slots, tile, _ = tile_vals.shape
    hid = recur_weight.shape[0]
    _, rows, total_steps, _ = hidden_grad.shape
    bf16, f32 = jnp.bfloat16, jnp.float32

    flat = tile_cols.reshape(1, steps, row_blocks * slots)
    low = jnp.arange(nv, dtype=jnp.int32)[:, None, None] * row_blocks
    named = jnp.where((flat >= low) & (flat < low + row_blocks), flat - low, 0)
    request = jnp.max(named, axis=2)
    request = jnp.pad(request, ((0, 0), (0, -steps % 8)))
    request = jnp.broadcast_to(request[:, :, None], request.shape + (LANES,))

    live = lax.broadcasted_iota(jnp.int32, tile_cols.shape, 2) < tile_count[:, :, None]
    places = jnp.where(live, tile_cols // row_blocks, nv)

    def padded(count, unit):
        unit = unit * ns * nv
        return -(-count // unit) * unit

    rows1 = padded(4 * (width + hid), 16)
    rows2 = padded(width + 5, 8)
    most = max(ns, nv)
    dma = pltpu.SemaphoreType.DMA

    def reduction(count, kept):
        part = count // ns
        return [
            pltpu.VMEM((count, LANES), f32),
            pltpu.VMEM((ns - 1, part, LANES), f32),
            pltpu.VMEM((part, LANES), f32),
            pltpu.VMEM((nv - 1, part // nv, LANES), f32),
            pltpu.VMEM((count, LANES), kept),
        ]

    scratch = [
        pltpu.VMEM(tile_vals.shape, bf16),
        pltpu.VMEM((nv,) + request.shape[1:], jnp.int32),
        pltpu.VMEM((nv, steps, tile, width), bf16),
        pltpu.VMEM((nv + 1, steps, tile, width), bf16),
        pltpu.VMEM((steps, verts, width), bf16),
        pltpu.VMEM((steps, verts, width), f32),
        pltpu.VMEM((steps, verts, width), bf16),
        pltpu.VMEM((total_steps, rows, width), bf16),
        pltpu.VMEM((total_steps + 1, rows, hid), bf16),
        pltpu.VMEM((total_steps, 4, rows, hid), f32),
        pltpu.VMEM((total_steps + 1, rows, hid), f32),
        pltpu.VMEM((total_steps, rows, width), bf16),
        pltpu.VMEM((steps, verts, width), bf16),
        pltpu.VMEM((rows, hid), f32),
        pltpu.VMEM((rows, hid), f32),
        pltpu.VMEM((width + hid, 4 * hid), bf16),
        pltpu.VMEM((4 * hid, width + hid), bf16),
        pltpu.VMEM((8, 4 * hid), f32),
        *reduction(rows1, bf16),
        *reduction(rows2, f32),
        dma,
        dma((2, nv)),
        dma((2, nv)),
        dma((2, ns, steps)),
        dma((total_steps,)),
        dma((ns, steps)),
        dma((8, most)),
        dma((8, most)),
    ]
    vmem = pl.BlockSpec(memory_space=pltpu.VMEM)
    smem = pl.BlockSpec(memory_space=pltpu.SMEM)
    hidden, grad_gcn, grad_gbias, grad_input, grad_recur, grad_bias = pl.pallas_call(
        functools.partial(kernel, sizes),
        out_shape=[
            jax.ShapeDtypeStruct((total_steps, rows, hid), bf16),
            jax.ShapeDtypeStruct((width, width), f32),
            jax.ShapeDtypeStruct((1, width), f32),
            jax.ShapeDtypeStruct((width, 4 * hid), f32),
            jax.ShapeDtypeStruct((hid, 4 * hid), f32),
            jax.ShapeDtypeStruct((1, 4 * hid), f32),
        ],
        in_specs=[vmem, smem, vmem, pl.BlockSpec(memory_space=pl.ANY)] + [vmem] * 6,
        out_specs=[vmem] * 6,
        scratch_shapes=scratch,
        compiler_params=pltpu.CompilerParams(
            collective_id=0, has_side_effects=True, vmem_limit_bytes=48 * 2**20
        ),
    )(
        request,
        places,
        features.reshape(steps, row_blocks, tile, width),
        tile_vals,
        gcn_weight,
        gcn_bias.reshape(1, -1),
        input_weight,
        recur_weight,
        lstm_bias.reshape(1, -1),
        jnp.transpose(hidden_grad[0], (1, 0, 2)),
    )
    hidden_states = jnp.transpose(hidden, (1, 0, 2))[None]
    return (
        hidden_states,
        grad_gcn,
        grad_gbias.reshape(-1),
        grad_input,
        grad_recur,
        grad_bias.reshape(-1),
    )


def solution(mesh):
    sizes = {axis: mesh.shape[axis] for axis in ("snap", "vtx")}
    return jax.shard_map(
        functools.partial(on_device, sizes),
        mesh=mesh,
        in_specs=(
            P("snap", "vtx", None),
            P("snap", "vtx", None, None, None),
            P("snap", "vtx", None),
            P("snap", "vtx"),
            P(),
            P(),
            P(),
            P(),
            P(),
            P("vtx", "snap", None, None),
        ),
        out_specs=(P("vtx", "snap", None, None), P(), P(), P(), P(), P()),
        check_vma=False,
    )
```

time: 332 us -> 72.3 us (0.22)
  waiting for transfers between devices: 177 us -> 0 us
  Pallas kernels: 0 us -> 59 us
  blocking collectives: 38.7 us -> 0 us
  matrix products: 33 us -> 0 us
  other arithmetic: 32.8 us -> 0.97 us
  local copies, waits for them, and re-layouts: 27 us -> 11.2 us
  between operations: 14.3 us -> 0.67 us
  starting transfers between devices: 7.02 us -> 0 us
    psum x1 -> x0, waiting for transfers between devices: 86.2 us -> none  [on_device(): lax.psum((grad_gcn, grad_gbias, grad_input, grad_recur, grad_bias), ('sna...]
    all_gather x1 -> x0, waiting for transfers between devices: 76.8 us -> none  [on_device(): gathered = lax.all_gather(features, 'vtx', axis=1, tiled=True)]
    pallas_call x0 -> x1, Pallas kernels: none -> 59 us  [on_device(): pl.pallas_call(functools.partial(kernel, sizes), out_shape=[jax.ShapeDtyp...]
    psum x1 -> x0, blocking collectives: 38.7 us -> none  [on_device(): lax.psum((grad_gcn, grad_gbias, grad_input, grad_recur, grad_bias), ('sna...]
    dot_general x23 -> x0, matrix products: 33 us -> none  [the longest x8 16.5 us: advance(): jnp.dot(last_out, recur_weight, preferred_element_type=jnp.float32)]
    another operation x16 -> x0, other arithmetic: 22.8 us -> none
    all_to_all x2 -> x0, waiting for transfers between devices: 13.1 us -> none  [the longest x1 7.67 us: on_device(): lax.all_to_all(layer_out, 'snap', split_axis=1, concat_axis=0, tiled=True)]
    squeeze x8 -> x0, local copies, waits for them, and re-layouts: 8.64 us -> none  [on_device(): _, (all_pre, all_cells, all_outs) = lax.scan(advance, start, input_gates)]
  transfers between devices with their start and end apart: 4 -> 0, of which waited for: 4 -> 0; matrix products, arithmetic and copies ran while one was open for 2% -> 0% of each run, Pallas kernels for 0% -> 0%
where the time goes in v1:
time: 72.3 us; the launch traced here: 71.9 us
  Pallas kernels  59 us (82%)
  local copies, waits for them, and re-layouts  11.2 us (15%)
  other arithmetic  0.97 us (1%)
    pallas_call x1, Pallas kernels, on_device(): pl.pallas_call(functools.partial(kernel, sizes), out_shape=[jax.ShapeDtyp...  59 us
    unnamed x20, local copies, waits for them, and re-layouts  10.4 us

profile of v1, /device:TPU:0, one launch (start us, length us, event | category | flops | bytes accessed | tf_op | source)
XLA Modules:
  0.0 71.9 jit_solution(13091551085206671027)
XLA Ops:
  0.6 0.8 %ge.17 = s32[2,64]{1,0:T(2,128)S(1)} reshape(s32[2,8,8]{2,1,0:T(8,128)} %param.12) | data formatting | bytes 1024 | tf_op jit(solution)/shard_map/ge | solution.py:408
  1.4 0.2 select_reduce_fusion
  1.6 0.1 copy.21
  1.7 0.8 %fusion.1.place_ref = s32[2,8,8]{2,1,0:T(8,128)S(1)} fusion(s32[2,8,8]{2,1,0:T(8,128)} %param.12, s32[2,8]{1,0:T(2,128)} %param.13), kind=kLoop, calls=%fused_computation.6 | loop fusion | flops 2176 | bytes 1088 | tf_op jit(solution)/shard_map/jit(_where)/select_n | solution.py:414
  2.5 0.1 broadcast_in_dim.18.request_ref
  2.5 1.1 %copy.23 = bf16[1,256,8,128]{3,1,2,0:T(8,128)(2,1)S(1)} copy(bf16[1,256,8,128]{3,2,1,0:T(8,128)(2,1)} %param.19) | data formatting | bytes 1048576 | tf_op args[9]
  3.7 0.0 copy-start
  3.7 1.0 %copy-done = bf16[2,1024,128]{2,1,0:T(8,128)(2,1)S(1)} copy-done((bf16[2,1024,128]{2,1,0:T(8,128)(2,1)S(1)}, bf16[2,1024,128]{2,1,0:T(8,128)(2,1)}, u32[]{:S(2)}) %copy-start) | copy-done | bytes 524312
  4.7 0.0 copy-start.1
  4.7 0.9 %copy-done.1 = bf16[128,512]{1,0:T(8,128)(2,1)S(1)} copy-done((bf16[128,512]{1,0:T(8,128)(2,1)S(1)}, bf16[128,512]{1,0:T(8,128)(2,1)}, u32[]{:S(2)}) %copy-start.1) | copy-done | bytes 131096
  5.6 0.9 %copy-done.2 = bf16[128,512]{1,0:T(8,128)(2,1)S(1)} copy-done((bf16[128,512]{1,0:T(8,128)(2,1)S(1)}, bf16[128,512]{1,0:T(8,128)(2,1)}, u32[]{:S(2)}) %copy-start.2) | copy-done | bytes 131096
  6.5 0.0 copy-start.3
  6.5 0.8 %copy-done.3 = bf16[128,128]{1,0:T(8,128)(2,1)S(1)} copy-done((bf16[128,128]{1,0:T(8,128)(2,1)S(1)}, bf16[128,128]{1,0:T(8,128)(2,1)}, u32[]{:S(2)}) %copy-start.3) | copy-done | bytes 32792
  7.3 0.0 copy-start.4
  7.3 0.7 copy-done.4
  8.0 0.0 copy-start.5
  8.0 0.7 copy-done.5
  8.6 59.0 %shard_map.145 = (bf16[8,256,128]{2,1,0:T(8,128)(2,1)S(1)}, f32[128,128]{1,0:T(8,128)S(1)}, f32[1,128]{1,0:T(1,128)S(1)}, f32[128,512]{1,0:T(8,128)S(1)}, f32[128,512]{1,0:T(8,128)S(1)}, /*index=5*/f32[1,512]{1,0:T(1,128)S(1)}) custom-call(s32[8,8,128]{2,1,0:T(8,128)S(1)} %broadcast_in_dim.18.request_ref, s32[2,8,8]{2,1,0:T(8,128)S(1)} %fusion.1.place_ref, ...), custom_call_target="tpu_custom_call" | custom-call | tf_op jit(solution)/shard_map/pallas_call | solution.py:467
  67.6 1.1 %copy.20 = bf16[1,256,8,128]{3,2,1,0:T(8,128)(2,1)} copy(bf16[1,256,8,128]{3,1,2,0:T(8,128)(2,1)S(1)} %bitcast.14) | data formatting | bytes 1048576
  68.8 0.6 copy.29
  69.4 0.5 copy.30
  69.9 0.7 copy.31
  70.6 0.7 copy.32
  71.3 0.6 copy.33
  (3 shorter events, 0.0 us)
Async XLA Ops:
  3.7 1.0 %copy-start = (bf16[2,1024,128]{2,1,0:T(8,128)(2,1)S(1)}, bf16[2,1024,128]{2,1,0:T(8,128)(2,1)}, u32[]{:S(2)}) copy-start(bf16[2,1024,128]{2,1,0:T(8,128)(2,1)} %param.10) | copy-start | bytes 1572868
  4.7 0.9 %copy-start.1 = (bf16[128,512]{1,0:T(8,128)(2,1)S(1)}, bf16[128,512]{1,0:T(8,128)(2,1)}, u32[]{:S(2)}) copy-start(bf16[128,512]{1,0:T(8,128)(2,1)} %in_w_ref.1) | copy-start | bytes 393220
  5.6 0.9 %copy-start.2 = (bf16[128,512]{1,0:T(8,128)(2,1)S(1)}, bf16[128,512]{1,0:T(8,128)(2,1)}, u32[]{:S(2)}) copy-start(bf16[128,512]{1,0:T(8,128)(2,1)} %rec_w_ref.1) | copy-start | bytes 393220
  6.5 0.8 %copy-start.3 = (bf16[128,128]{1,0:T(8,128)(2,1)S(1)}, bf16[128,128]{1,0:T(8,128)(2,1)}, u32[]{:S(2)}) copy-start(bf16[128,128]{1,0:T(8,128)(2,1)} %gcn_w_ref.1) | copy-start | bytes 98308
  7.3 0.7 copy-start.4
  8.0 0.7 copy-start.5

commit v2 on v1

--- a/solution.py
+++ b/solution.py
@@ -81,16 +81,16 @@
 
 def kernel(
     sizes,
-    request_ref,
+    request_hbm,
     place_ref,
-    feat_ref,
+    feat_hbm,
     tiles_ref,
-    gcn_w_ref,
-    gcn_b_ref,
-    in_w_ref,
-    rec_w_ref,
-    lstm_b_ref,
-    hgrad_ref,
+    gcn_w_hbm,
+    gcn_b_hbm,
+    in_w_hbm,
+    rec_w_hbm,
+    lstm_b_hbm,
+    hgrad_hbm,
     hid_out,
     gcn_out,
     gcn_b_out,
@@ -98,6 +98,12 @@
     rec_out,
     lstm_b_out,
     tiles,
+    request_ref,
+    feat_ref,
+    gcn_w_ref,
+    gcn_b_ref,
+    lstm_b_ref,
+    hgrad_ref,
     asked,
     staged,
     fetched,
@@ -125,7 +131,7 @@
     part2,
     chunk_in2,
     whole2,
-    tile_sem,
+    load_sem,
     ask_sem,
     feat_sem,
     layer_sem,
@@ -156,11 +162,27 @@
         for k in range(1, sizes[axis]):
             peer = lax.rem(me[axis] + k, sizes[axis])
             pl.semaphore_signal(barrier, inc=1, device_id={axis: peer}, device_id_type=MESH)
-    load_tiles = pltpu.make_async_copy(tiles_ref, tiles, tile_sem)
-    load_tiles.start()
-    fetched[nv] = jnp.zeros((steps, tile, width), jnp.bfloat16)
-    weights[...] = jnp.concatenate([in_w_ref[...], rec_w_ref[...]], axis=0)
-    weights_t[...] = weights[...].T
+    loads = [
+        pltpu.make_async_copy(src, dst, load_sem.at[n])
+        for n, (src, dst) in enumerate(
+            [
+                (request_hbm, request_ref),
+                (feat_hbm, feat_ref),
+                (tiles_ref, tiles),
+                (in_w_hbm, weights.at[pl.ds(0, width)]),
+                (rec_w_hbm, weights.at[pl.ds(width, hid)]),
+                (gcn_w_hbm, gcn_w_ref),
+                (gcn_b_hbm, gcn_b_ref),
+                (lstm_b_hbm, lstm_b_ref),
+                (hgrad_hbm, hgrad_ref),
+            ]
+        )
+    ]
+    for load in loads:
+        load.start()
+    for s in range(steps):
+        fetched[s][nv] = jnp.zeros((tile, width), jnp.bfloat16)
+    loads[0].wait()
     pl.semaphore_wait(barrier, ns + nv - 2)
 
     def ask(k, forward):
@@ -169,31 +191,41 @@
             request_ref.at[peer], asked.at[k], ask_sem.at[0, k], ask_sem.at[1, k], "vtx", peer
         )
 
-    def give(k, forward):
+    def give(k, s, forward):
         peer = lax.rem(me_v + k, nv) if forward else lax.rem(me_v - k + nv, nv)
         return remote(
-            staged.at[k],
-            fetched.at[me_v if forward else peer],
-            feat_sem.at[0, k],
-            feat_sem.at[1, k],
+            staged.at[k, s],
+            fetched[s].at[me_v if forward else peer],
+            feat_sem.at[0, k, s],
+            feat_sem.at[1, k, s],
             "vtx",
             peer,
         )
 
     for k in range(1, nv):
         ask(k, True).start()
-    own_request = request_ref[me_v]
-    for s in range(steps):
-        fetched[me_v, s] = feat_ref[s, own_request[s, 0]]
+    loads[1].wait()
     for k in range(1, nv):
         ask(nv - k, False).wait_recv()
         wanted = asked[nv - k]
-        for s in range(steps):
+        staged[k, 0] = feat_ref[0, wanted[0, 0]]
+        give(k, 0, True).start()
+        for s in range(1, steps):
             staged[k, s] = feat_ref[s, wanted[s, 0]]
-        give(k, True).start()
-    for k in range(1, nv):
-        give(k, False).wait_recv()
-    load_tiles.wait()
+    own_request = request_ref[me_v]
+    for s in range(steps):
+        fetched[s][me_v] = feat_ref[s, own_request[s, 0]]
+    for load in loads[2:]:
+        load.wait()
+    weights_t[...] = weights[...].T
+
+    def give_next(s):
+        for k in range(1, nv):
+            give(k, s - 1, True).wait_send()
+            give(k, s, True).start()
+
+    if steps > 1:
+        give_next(1)
 
     def layer_copy(k, s, forward):
         peer = lax.rem(me_s + k, ns) if forward else lax.rem(me_s - k + ns, ns)
@@ -207,9 +239,13 @@
             peer,
         )
 
-    def convolve(s, carry):
+    def convolve(s):
+        for k in range(1, nv):
+            give(k, s, False).wait_recv()
+        if 0 < s < steps - 1:
+            give_next(s + 1)
         for r in range(row_blocks):
-            picked = [fetched[place_ref[s, r, m], s] for m in range(slots)]
+            picked = [fetched[s][place_ref[s, r, m]] for m in range(slots)]
             left = jnp.concatenate([tiles[s, r, m] for m in range(slots)], axis=1)
             summed = jnp.dot(
                 left, jnp.concatenate(picked, axis=0), preferred_element_type=jnp.float32
@@ -224,9 +260,9 @@
         for k in range(1, ns):
             layer_copy(k, s, True).start()
         xs[me_s * steps + s] = layer[s, pl.ds(pl.multiple_of(me_s * rows, rows), rows), :]
-        return carry
-
-    lax.fori_loop(0, steps, convolve, 0)
+
+    for s in range(steps):
+        convolve(s)
 
     hs[0] = jnp.zeros((rows, hid), jnp.bfloat16)
     cells[0] = jnp.zeros((rows, hid), jnp.float32)
@@ -366,7 +402,7 @@
 
     for k in range(1, nv):
         ask(k, True).wait_send()
-        give(k, True).wait_send()
+        give(k, steps - 1, True).wait_send()
     for k in range(1, ns):
         for s in range(steps):
             layer_copy(k, s, True).wait_send()
@@ -381,6 +417,19 @@
     lax.fori_loop(0, total_steps, drain, 0)
     first.drain()
     second.drain()
+
+
+def write_out(*refs):
+    *arrays, sems = refs
+    half = len(arrays) // 2
+    copies = [
+        pltpu.make_async_copy(src, dst, sems.at[n])
+        for n, (src, dst) in enumerate(zip(arrays[:half], arrays[half:]))
+    ]
+    for copy in copies:
+        copy.start()
+    for copy in copies:
+        copy.wait()
 
 
 def on_device(
@@ -403,10 +452,10 @@
     _, rows, total_steps, _ = hidden_grad.shape
     bf16, f32 = jnp.bfloat16, jnp.float32
 
-    flat = tile_cols.reshape(1, steps, row_blocks * slots)
-    low = jnp.arange(nv, dtype=jnp.int32)[:, None, None] * row_blocks
-    named = jnp.where((flat >= low) & (flat < low + row_blocks), flat - low, 0)
-    request = jnp.max(named, axis=2)
+    blocks = tile_cols[None]
+    low = lax.broadcasted_iota(jnp.int32, (nv,) + tile_cols.shape, 0) * row_blocks
+    named = jnp.where((blocks >= low) & (blocks < low + row_blocks), blocks - low, 0)
+    request = jnp.max(named, axis=(2, 3))
     request = jnp.pad(request, ((0, 0), (0, -steps % 8)))
     request = jnp.broadcast_to(request[:, :, None], request.shape + (LANES,))
 
@@ -434,9 +483,15 @@
 
     scratch = [
         pltpu.VMEM(tile_vals.shape, bf16),
+        pltpu.VMEM(request.shape, jnp.int32),
+        pltpu.VMEM((steps, row_blocks, tile, width), bf16),
+        pltpu.VMEM(gcn_weight.shape, bf16),
+        pltpu.VMEM((1, width), f32),
+        pltpu.VMEM((1, 4 * hid), f32),
+        pltpu.VMEM((total_steps, rows, hid), bf16),
         pltpu.VMEM((nv,) + request.shape[1:], jnp.int32),
         pltpu.VMEM((nv, steps, tile, width), bf16),
-        pltpu.VMEM((nv + 1, steps, tile, width), bf16),
+        [pltpu.VMEM((nv + 1, tile, width), bf16) for _ in range(steps)],
         pltpu.VMEM((steps, verts, width), bf16),
         pltpu.VMEM((steps, verts, width), f32),
         pltpu.VMEM((steps, verts, width), bf16),
@@ -453,9 +508,9 @@
         pltpu.VMEM((8, 4 * hid), f32),
         *reduction(rows1, bf16),
         *reduction(rows2, f32),
-        dma,
+        dma((9,)),
         dma((2, nv)),
-        dma((2, nv)),
+        dma((2, nv, steps)),
         dma((2, ns, steps)),
         dma((total_steps,)),
         dma((ns, steps)),
@@ -464,7 +519,8 @@
     ]
     vmem = pl.BlockSpec(memory_space=pltpu.VMEM)
     smem = pl.BlockSpec(memory_space=pltpu.SMEM)
-    hidden, grad_gcn, grad_gbias, grad_input, grad_recur, grad_bias = pl.pallas_call(
+    hbm = pl.BlockSpec(memory_space=pl.ANY)
+    hidden, *grads = pl.pallas_call(
         functools.partial(kernel, sizes),
         out_shape=[
             jax.ShapeDtypeStruct((total_steps, rows, hid), bf16),
@@ -474,11 +530,11 @@
             jax.ShapeDtypeStruct((hid, 4 * hid), f32),
             jax.ShapeDtypeStruct((1, 4 * hid), f32),
         ],
-        in_specs=[vmem, smem, vmem, pl.BlockSpec(memory_space=pl.ANY)] + [vmem] * 6,
+        in_specs=[hbm, smem] + [hbm] * 8,
         out_specs=[vmem] * 6,
         scratch_shapes=scratch,
         compiler_params=pltpu.CompilerParams(
-            collective_id=0, has_side_effects=True, vmem_limit_bytes=48 * 2**20
+            collective_id=0, has_side_effects=True, vmem_limit_bytes=60 * 2**20
         ),
     )(
         request,
@@ -492,6 +548,13 @@
         lstm_bias.reshape(1, -1),
         jnp.transpose(hidden_grad[0], (1, 0, 2)),
     )
+    grad_gcn, grad_gbias, grad_input, grad_recur, grad_bias = pl.pallas_call(
+        write_out,
+        out_shape=[jax.ShapeDtypeStruct(grad.shape, f32) for grad in grads],
+        in_specs=[hbm] * len(grads),
+        out_specs=[hbm] * len(grads),
+        scratch_shapes=[dma((len(grads),))],
+    )(*grads)
     hidden_states = jnp.transpose(hidden, (1, 0, 2))[None]
     return (
         hidden_states,

time: 72.3 us -> 86.9 us (1.20)
  Pallas kernels: 59 us -> 78.6 us
  local copies, waits for them, and re-layouts: 11.2 us -> 4.77 us
  other arithmetic: 0.97 us -> 2.51 us
    pallas_call x0 -> x1, Pallas kernels: none -> 19.1 us  [on_device(): pl.pallas_call(write_out, out_shape=[jax.ShapeDtypeStruct(grad.shape, f32...]
    unnamed x20 -> x2, local copies, waits for them, and re-layouts: 10.4 us -> 4.08 us
    reduce_max x1, other arithmetic: 0.18 us -> 1.14 us  [on_device(): request = jnp.max(named, axis=(2, 3))]
where the time goes in v2:
time: 86.9 us; the launch traced here: 86.5 us
  Pallas kernels  78.6 us (90%)
  local copies, waits for them, and re-layouts  4.77 us (5%)
  other arithmetic  2.51 us (3%)
    pallas_call x1, Pallas kernels, on_device(): pl.pallas_call(functools.partial(kernel, sizes), out_shape=[jax.ShapeDtyp...  59.5 us
    pallas_call x1, Pallas kernels, on_device(): pl.pallas_call(write_out, out_shape=[jax.ShapeDtypeStruct(grad.shape, f32...  19.1 us
    unnamed x2, local copies, waits for them, and re-layouts  4.08 us

profile of v2, /device:TPU:0, one launch (start us, length us, event | category | flops | bytes accessed | tf_op | source)
XLA Modules:
  0.0 86.5 jit_solution(2165206695013159865)
XLA Ops:
  0.6 1.1 %select_reduce_fusion = s32[8,2]{1,0:T(8,128)S(1)} fusion(s32[2,8,8]{2,1,0:T(8,128)} %param.12, s32[8]{0:T(128)S(1)} %get-tuple-element.41, s32[8]{0:T(128)S(1)} %get-tuple-element.40), kind=kLoop, calls=%fused_computation.1 | loop fusion | flops 6128 | bytes 640 | tf_op jit(solution)/shard_map/reduce_max | solution.py:458
  1.8 1.4 %fusion.1.place_ref = s32[2,8,8]{2,1,0:T(8,128)} fusion(s32[2,8,8]{2,1,0:T(8,128)} %param.12, s32[2,8]{1,0:T(2,128)} %param.13), kind=kLoop, calls=%fused_computation.7 | loop fusion | flops 2176 | bytes 1088 | tf_op jit(solution)/shard_map/jit(_where)/select_n | solution.py:463
  3.2 0.7 broadcast_in_dim.18.request_hbm
  3.9 1.9 %copy.21 = bf16[1,256,8,128]{3,1,2,0:T(8,128)(2,1)} copy(bf16[1,256,8,128]{3,2,1,0:T(8,128)(2,1)} %param.19) | data formatting | bytes 1048576 | tf_op args[9]
  5.8 59.5 %shard_map.145 = (bf16[8,256,128]{2,1,0:T(8,128)(2,1)}, f32[128,128]{1,0:T(8,128)}, f32[1,128]{1,0:T(1,128)}, f32[128,512]{1,0:T(8,128)}, f32[128,512]{1,0:T(8,128)}, /*index=5*/f32[1,512]{1,0:T(1,128)}) custom-call(s32[8,8,128]{2,1,0:T(8,128)} %broadcast_in_dim.18.request_hbm, s32[2,8,8]{2,1,0:T(8,128)} %fusion.1.place_ref, ...), custom_call_target="tpu_custom_call" | custom-call | tf_op jit(solution)/shard_map/pallas_call | solution.py:523
  65.2 2.2 %copy.19 = bf16[1,256,8,128]{3,2,1,0:T(8,128)(2,1)} copy(bf16[1,256,8,128]{3,1,2,0:T(8,128)(2,1)} %bitcast.14) | data formatting | bytes 1048576
  67.4 19.1 %shard_map.146 = (f32[128,128]{1,0:T(8,128)}, f32[1,128]{1,0:T(1,128)}, f32[128,512]{1,0:T(8,128)}, f32[128,512]{1,0:T(8,128)}, f32[1,512]{1,0:T(1,128)}) custom-call(f32[128,128]{1,0:T(8,128)} %get-tuple-element.18.refs_0_, f32[1,128]{1,0:T(1,128)} %get-tuple-element.19.refs_1_, f32[128,512]{1,0:T(8,128)} %get-tuple-element.20.refs_2_, ...), custom_call_target="tpu_custom_call" | custom-call | tf_op jit(solution)/shard_map/pallas_call | solution.py:551
  (2 shorter events, 0.0 us)

commit v3 on v2

--- a/solution.py
+++ b/solution.py
@@ -16,9 +16,10 @@
 
 
 class Reducer:
-    def __init__(self, me, sizes, own, part_in, part_sum, chunk_in, whole, sems):
+    def __init__(self, me, sizes, own, sent, part_in, part_sum, part_sent, chunk_in, whole, sems):
         self.me, self.sizes = me, sizes
-        self.own, self.part_in, self.part_sum = own, part_in, part_sum
+        self.own, self.sent, self.part_in = own, sent, part_in
+        self.part_sum, self.part_sent = part_sum, part_sent
         self.chunk_in, self.whole, self.sems = chunk_in, whole, sems
         self.part = part_sum.shape[0]
         self.chunk = self.part // sizes["vtx"]
@@ -33,10 +34,10 @@
         n, me = self.sizes[axis], self.me[axis]
         peer = lax.rem(me + k, n) if forward else lax.rem(me - k + n, n)
         if stage == 0:
-            src, dst = self.own.at[self.rows(peer)], self.part_in.at[k - 1]
+            src, dst = self.sent.at[self.rows(peer)], self.part_in.at[k - 1]
         elif stage == 1:
             here = pl.ds(pl.multiple_of(peer * self.chunk, self.chunk), self.chunk)
-            src, dst = self.part_sum.at[here], self.chunk_in.at[k - 1]
+            src, dst = self.part_sent.at[here], self.chunk_in.at[k - 1]
         elif stage == 2:
             src = dst = self.whole.at[self.rows(self.me["snap"], me if forward else peer)]
         else:
@@ -65,6 +66,8 @@
             for k in self.peers(stage):
                 total = total + self.part_in[k - 1].astype(jnp.float32)
             self.part_sum[...] = total
+            if self.part_sent is not self.part_sum:
+                self.part_sent[...] = total.astype(self.part_sent.dtype)
         elif stage == 1:
             here = pl.ds(pl.multiple_of(self.me["vtx"] * self.chunk, self.chunk), self.chunk)
             total = self.part_sum[here, :]
@@ -81,7 +84,7 @@
 
 def kernel(
     sizes,
-    request_hbm,
+    cols_hbm,
     place_ref,
     feat_hbm,
     tiles_ref,
@@ -98,12 +101,14 @@
     rec_out,
     lstm_b_out,
     tiles,
+    cols_ref,
     request_ref,
     feat_ref,
     gcn_w_ref,
     gcn_b_ref,
     lstm_b_ref,
     hgrad_ref,
+    hgrad,
     asked,
     staged,
     fetched,
@@ -126,6 +131,8 @@
     part1,
     chunk_in1,
     whole1,
+    sent1,
+    part_sent1,
     sum2,
     part_in2,
     part2,
@@ -145,7 +152,7 @@
     me = {"snap": me_s, "vtx": me_v}
     steps, verts, width = layer.shape
     _, row_blocks, slots, tile, _ = tiles_ref.shape
-    total_steps, rows, hid = hgrad_ref.shape
+    rows, total_steps, hid = hgrad_ref.shape
 
     def remote(src, dst, send, recv, axis, peer):
         return pltpu.make_async_remote_copy(
@@ -166,7 +173,7 @@
         pltpu.make_async_copy(src, dst, load_sem.at[n])
         for n, (src, dst) in enumerate(
             [
-                (request_hbm, request_ref),
+                (cols_hbm, cols_ref),
                 (feat_hbm, feat_ref),
                 (tiles_ref, tiles),
                 (in_w_hbm, weights.at[pl.ds(0, width)]),
@@ -174,7 +181,7 @@
                 (gcn_w_hbm, gcn_w_ref),
                 (gcn_b_hbm, gcn_b_ref),
                 (lstm_b_hbm, lstm_b_ref),
-                (hgrad_hbm, hgrad_ref),
+                (hgrad_hbm.at[0], hgrad_ref),
             ]
         )
     ]
@@ -183,6 +190,12 @@
     for s in range(steps):
         fetched[s][nv] = jnp.zeros((tile, width), jnp.bfloat16)
     loads[0].wait()
+    for p in range(nv):
+        blocks = cols_ref[...] - p * row_blocks
+        named = jnp.where((blocks >= 0) & (blocks < row_blocks), blocks, 0)
+        for s in range(steps):
+            block = jnp.max(named[s], axis=(0, 1), keepdims=True)
+            request_ref[p, s] = jnp.broadcast_to(block, (8, LANES))
     pl.semaphore_wait(barrier, ns + nv - 2)
 
     def ask(k, forward):
@@ -208,13 +221,13 @@
     for k in range(1, nv):
         ask(nv - k, False).wait_recv()
         wanted = asked[nv - k]
-        staged[k, 0] = feat_ref[0, wanted[0, 0]]
+        staged[k, 0] = feat_ref[0, wanted[0, 0, 0]]
         give(k, 0, True).start()
         for s in range(1, steps):
-            staged[k, s] = feat_ref[s, wanted[s, 0]]
+            staged[k, s] = feat_ref[s, wanted[s, 0, 0]]
     own_request = request_ref[me_v]
     for s in range(steps):
-        fetched[s][me_v] = feat_ref[s, own_request[s, 0]]
+        fetched[s][me_v] = feat_ref[s, own_request[s, 0, 0]]
     for load in loads[2:]:
         load.wait()
     weights_t[...] = weights[...].T
@@ -226,6 +239,7 @@
 
     if steps > 1:
         give_next(1)
+    hgrad[...] = hgrad_ref[...].astype(jnp.float32).reshape(rows * total_steps, hid)
 
     def layer_copy(k, s, forward):
         peer = lax.rem(me_s + k, ns) if forward else lax.rem(me_s - k + ns, ns)
@@ -318,7 +332,7 @@
         t = total_steps - 1 - step
         gate_in, gate_keep, gate_new, gate_out = (acts[t, q] for q in range(4))
         squash = jnp.tanh(cells[t + 1])
-        dh = hgrad_ref[t].astype(jnp.float32) + back[...]
+        dh = hgrad[pl.ds(t, rows, stride=total_steps), :] + back[...]
         dc = dcell[...] + dh * gate_out * (1.0 - squash * squash)
         dgates = jnp.concatenate(
             [
@@ -358,8 +372,13 @@
 
     lax.fori_loop(0, total_steps, retreat, 0)
 
-    first = Reducer(me, sizes, sum1, part_in1, part1, chunk_in1, whole1, sems1)
-    second = Reducer(me, sizes, sum2, part_in2, part2, chunk_in2, whole2, sems2)
+    first = Reducer(
+        me, sizes, sum1, sent1, part_in1, part1, part_sent1, chunk_in1, whole1, sems1
+    )
+    second = Reducer(
+        me, sizes, sum2, sum2, part_in2, part2, part2, chunk_in2, whole2, sems2
+    )
+    sent1[...] = sum1[...].astype(jnp.bfloat16)
     first.start(0)
 
     sum2[...] = jnp.zeros(sum2.shape, jnp.float32)
@@ -421,14 +440,16 @@
 
 def write_out(*refs):
     *arrays, sems = refs
-    half = len(arrays) // 2
-    copies = [
-        pltpu.make_async_copy(src, dst, sems.at[n])
-        for n, (src, dst) in enumerate(zip(arrays[:half], arrays[half:]))
-    ]
-    for copy in copies:
+    n = len(arrays) // 3
+    srcs, dsts, held = arrays[:n], arrays[n : 2 * n], arrays[2 * n :]
+    ins = [pltpu.make_async_copy(srcs[i], held[i], sems.at[0, i]) for i in range(n)]
+    outs = [pltpu.make_async_copy(held[i], dsts[i], sems.at[1, i]) for i in range(n)]
+    for copy in ins:
         copy.start()
-    for copy in copies:
+    for copy_in, copy_out in zip(ins, outs):
+        copy_in.wait()
+        copy_out.start()
+    for copy in outs:
         copy.wait()
 
 
@@ -452,13 +473,6 @@
     _, rows, total_steps, _ = hidden_grad.shape
     bf16, f32 = jnp.bfloat16, jnp.float32
 
-    blocks = tile_cols[None]
-    low = lax.broadcasted_iota(jnp.int32, (nv,) + tile_cols.shape, 0) * row_blocks
-    named = jnp.where((blocks >= low) & (blocks < low + row_blocks), blocks - low, 0)
-    request = jnp.max(named, axis=(2, 3))
-    request = jnp.pad(request, ((0, 0), (0, -steps % 8)))
-    request = jnp.broadcast_to(request[:, :, None], request.shape + (LANES,))
-
     live = lax.broadcasted_iota(jnp.int32, tile_cols.shape, 2) < tile_count[:, :, None]
     places = jnp.where(live, tile_cols // row_blocks, nv)
 
@@ -475,21 +489,23 @@
         part = count // ns
         return [
             pltpu.VMEM((count, LANES), f32),
-            pltpu.VMEM((ns - 1, part, LANES), f32),
+            pltpu.VMEM((ns - 1, part, LANES), kept),
             pltpu.VMEM((part, LANES), f32),
-            pltpu.VMEM((nv - 1, part // nv, LANES), f32),
+            pltpu.VMEM((nv - 1, part // nv, LANES), kept),
             pltpu.VMEM((count, LANES), kept),
         ]
 
     scratch = [
         pltpu.VMEM(tile_vals.shape, bf16),
-        pltpu.VMEM(request.shape, jnp.int32),
+        pltpu.VMEM(tile_cols.shape, jnp.int32),
+        pltpu.VMEM((nv, steps, 8, LANES), jnp.int32),
         pltpu.VMEM((steps, row_blocks, tile, width), bf16),
         pltpu.VMEM(gcn_weight.shape, bf16),
         pltpu.VMEM((1, width), f32),
         pltpu.VMEM((1, 4 * hid), f32),
-        pltpu.VMEM((total_steps, rows, hid), bf16),
-        pltpu.VMEM((nv,) + request.shape[1:], jnp.int32),
+        pltpu.VMEM((rows, total_steps, hid), bf16),
+        pltpu.VMEM((rows * total_steps, hid), f32),
+        pltpu.VMEM((nv, steps, 8, LANES), jnp.int32),
         pltpu.VMEM((nv, steps, tile, width), bf16),
         [pltpu.VMEM((nv + 1, tile, width), bf16) for _ in range(steps)],
         pltpu.VMEM((steps, verts, width), bf16),
@@ -507,6 +523,8 @@
         pltpu.VMEM((4 * hid, width + hid), bf16),
         pltpu.VMEM((8, 4 * hid), f32),
         *reduction(rows1, bf16),
+        pltpu.VMEM((rows1, LANES), bf16),
+        pltpu.VMEM((rows1 // ns, LANES), bf16),
         *reduction(rows2, f32),
         dma((9,)),
         dma((2, nv)),
@@ -537,7 +555,7 @@
             collective_id=0, has_side_effects=True, vmem_limit_bytes=60 * 2**20
         ),
     )(
-        request,
+        tile_cols,
         places,
         features.reshape(steps, row_blocks, tile, width),
         tile_vals,
@@ -546,14 +564,15 @@
         input_weight,
         recur_weight,
         lstm_bias.reshape(1, -1),
-        jnp.transpose(hidden_grad[0], (1, 0, 2)),
+        hidden_grad,
     )
     grad_gcn, grad_gbias, grad_input, grad_recur, grad_bias = pl.pallas_call(
         write_out,
         out_shape=[jax.ShapeDtypeStruct(grad.shape, f32) for grad in grads],
         in_specs=[hbm] * len(grads),
         out_specs=[hbm] * len(grads),
-        scratch_shapes=[dma((len(grads),))],
+        scratch_shapes=[pltpu.VMEM(grad.shape, f32) for grad in grads] + [dma((2, len(grads)))],
+        compiler_params=pltpu.CompilerParams(vmem_limit_bytes=60 * 2**20),
     )(*grads)
     hidden_states = jnp.transpose(hidden, (1, 0, 2))[None]
     return (

time: 86.9 us -> 64.2 us (0.74)
  Pallas kernels: 78.6 us -> 59.7 us
  local copies, waits for them, and re-layouts: 4.77 us -> 2.18 us
  other arithmetic: 2.51 us -> 1.37 us
    pallas_call x1, Pallas kernels: 19.1 us -> 1.87 us  [on_device(): pl.pallas_call(write_out, out_shape=[jax.ShapeDtypeStruct(grad.shape, f32...]
    unnamed x2 -> x1, local copies, waits for them, and re-layouts: 4.08 us -> 2.18 us
    pallas_call x1, Pallas kernels: 59.5 us -> 57.8 us  [on_device(): pl.pallas_call(functools.partial(kernel, sizes), out_shape=[jax.ShapeDtyp...]
    reduce_max x1 -> x0, other arithmetic: 1.14 us -> none  [on_device(): request = jnp.max(named, axis=(2, 3))]
where the time goes in v3:
time: 64.2 us; the launch traced here: 63.9 us
  Pallas kernels  59.7 us (93%)
  local copies, waits for them, and re-layouts  2.18 us (3%)
  other arithmetic  1.37 us (2%)
    pallas_call x1, Pallas kernels, on_device(): pl.pallas_call(functools.partial(kernel, sizes), out_shape=[jax.ShapeDtyp...  57.8 us
    unnamed x1, local copies, waits for them, and re-layouts  2.18 us
    pallas_call x1, Pallas kernels, on_device(): pl.pallas_call(write_out, out_shape=[jax.ShapeDtypeStruct(grad.shape, f32...  1.87 us
    select_n x1, other arithmetic, on_device(): places = jnp.where(live, tile_cols // row_blocks, nv)  1.37 us

profile of v3, /device:TPU:0, one launch (start us, length us, event | category | flops | bytes accessed | tf_op | source)
XLA Modules:
  0.0 63.9 jit_solution(9293096307267867615)
XLA Ops:
  0.6 1.4 %fusion.1.place_ref = s32[2,8,8]{2,1,0:T(8,128)} fusion(s32[2,8,8]{2,1,0:T(8,128)} %cols_hbm.1, s32[2,8]{1,0:T(2,128)} %param.13), kind=kLoop, calls=%fused_computation.5 | loop fusion | flops 2176 | bytes 1088 | tf_op jit(solution)/shard_map/jit(_where)/select_n | solution.py:477
  2.0 57.8 %shard_map.145 = (bf16[8,256,128]{2,1,0:T(8,128)(2,1)}, f32[128,128]{1,0:T(8,128)}, f32[1,128]{1,0:T(1,128)}, f32[128,512]{1,0:T(8,128)}, f32[128,512]{1,0:T(8,128)}, /*index=5*/f32[1,512]{1,0:T(1,128)}) custom-call(s32[2,8,8]{2,1,0:T(8,128)} %cols_hbm.1, s32[2,8,8]{2,1,0:T(8,128)} %fusion.1.place_ref, bf16[2,8,128,128]{3,2,1,0:T(8,128)(2,1)} %bitcast.9, ...), custom_call_target="tpu_custom_call" | custom-call | tf_op jit(solution)/shard_map/pallas_call | solution.py:541
  59.8 2.2 %copy.16 = bf16[1,256,8,128]{3,2,1,0:T(8,128)(2,1)} copy(bf16[1,256,8,128]{3,1,2,0:T(8,128)(2,1)} %bitcast.8) | data formatting | bytes 1048576
  62.0 1.9 %shard_map.146 = (f32[128,128]{1,0:T(8,128)}, f32[1,128]{1,0:T(1,128)}, f32[128,512]{1,0:T(8,128)}, f32[128,512]{1,0:T(8,128)}, f32[1,512]{1,0:T(1,128)}) custom-call(f32[128,128]{1,0:T(8,128)} %get-tuple-element.18.refs_0_, f32[1,128]{1,0:T(1,128)} %get-tuple-element.19.refs_1_, f32[128,512]{1,0:T(8,128)} %get-tuple-element.20.refs_2_, ...), custom_call_target="tpu_custom_call" | custom-call | tf_op jit(solution)/shard_map/pallas_call | solution.py:569

commit v4 on v3

--- a/solution.py
+++ b/solution.py
@@ -109,6 +109,7 @@
     lstm_b_ref,
     hgrad_ref,
     hgrad,
+    hidden,
     asked,
     staged,
     fetched,
@@ -278,6 +279,7 @@
     for s in range(steps):
         convolve(s)
 
+    piece = min(rows, LANES)
     hs[0] = jnp.zeros((rows, hid), jnp.bfloat16)
     cells[0] = jnp.zeros((rows, hid), jnp.float32)
 
@@ -289,21 +291,26 @@
             k = lax.rem(me_s - holder + ns, ns)
             layer_copy(k, lax.rem(t, steps), False).wait_recv()
 
-        both = jnp.concatenate([xs[t], hs[t]], axis=1)
-        gates = jnp.dot(both, weights[...], preferred_element_type=jnp.float32) + lstm_b_ref[...]
-        gate_in = sigmoid(gates[:, :hid])
-        gate_keep = sigmoid(gates[:, hid : 2 * hid])
-        gate_new = jnp.tanh(gates[:, 2 * hid : 3 * hid])
-        gate_out = sigmoid(gates[:, 3 * hid :])
-        cell = gate_keep * cells[t] + gate_in * gate_new
-        out = (gate_out * jnp.tanh(cell)).astype(jnp.bfloat16)
-        acts[t, 0] = gate_in
-        acts[t, 1] = gate_keep
-        acts[t, 2] = gate_new
-        acts[t, 3] = gate_out
-        cells[t + 1] = cell
-        hs[t + 1] = out
-        hid_out[t] = out
+        for at in range(0, rows, piece):
+            here = pl.ds(at, piece)
+            both = jnp.concatenate([xs[t, here, :], hs[t, here, :]], axis=1)
+            gates = (
+                jnp.dot(both, weights[...], preferred_element_type=jnp.float32) + lstm_b_ref[...]
+            )
+            gate_in = sigmoid(gates[:, :hid])
+            gate_keep = sigmoid(gates[:, hid : 2 * hid])
+            gate_new = jnp.tanh(gates[:, 2 * hid : 3 * hid])
+            gate_out = sigmoid(gates[:, 3 * hid :])
+            cell = gate_keep * cells[t, here, :] + gate_in * gate_new
+            out = (gate_out * jnp.tanh(cell)).astype(jnp.bfloat16)
+            acts[t, 0, here, :] = gate_in
+            acts[t, 1, here, :] = gate_keep
+            acts[t, 2, here, :] = gate_new
+            acts[t, 3, here, :] = gate_out
+            cells[t + 1, here, :] = cell
+            hs[t + 1, here, :] = out
+            place = pl.ds(t + at * total_steps, piece, stride=total_steps)
+            hidden[place, :] = out.astype(jnp.float32)
         return carry
 
     lax.fori_loop(0, total_steps, advance, 0)
@@ -330,23 +337,30 @@
 
     def retreat(step, carry):
         t = total_steps - 1 - step
-        gate_in, gate_keep, gate_new, gate_out = (acts[t, q] for q in range(4))
-        squash = jnp.tanh(cells[t + 1])
-        dh = hgrad[pl.ds(t, rows, stride=total_steps), :] + back[...]
-        dc = dcell[...] + dh * gate_out * (1.0 - squash * squash)
-        dgates = jnp.concatenate(
-            [
-                dc * gate_new * gate_in * (1.0 - gate_in),
-                dc * cells[t] * gate_keep * (1.0 - gate_keep),
-                dc * gate_in * (1.0 - gate_new * gate_new),
-                dh * squash * gate_out * (1.0 - gate_out),
-            ],
-            axis=1,
-        ).astype(jnp.bfloat16)
-        dcell[...] = dc * gate_keep
-        both_back = jnp.dot(dgates, weights_t[...], preferred_element_type=jnp.float32)
-        back[...] = both_back[:, width:]
-        grad = both_back[:, :width].astype(jnp.bfloat16)
+        parts, grads = [], []
+        for at in range(0, rows, piece):
+            here = pl.ds(at, piece)
+            gate_in, gate_keep, gate_new, gate_out = (acts[t, q, here, :] for q in range(4))
+            squash = jnp.tanh(cells[t + 1, here, :])
+            place = pl.ds(t + at * total_steps, piece, stride=total_steps)
+            dh = hgrad[place, :] + back[here, :]
+            dc = dcell[here, :] + dh * gate_out * (1.0 - squash * squash)
+            part = jnp.concatenate(
+                [
+                    dc * gate_new * gate_in * (1.0 - gate_in),
+                    dc * cells[t, here, :] * gate_keep * (1.0 - gate_keep),
+                    dc * gate_in * (1.0 - gate_new * gate_new),
+                    dh * squash * gate_out * (1.0 - gate_out),
+                ],
+                axis=1,
+            ).astype(jnp.bfloat16)
+            dcell[here, :] = dc * gate_keep
+            both_back = jnp.dot(part, weights_t[...], preferred_element_type=jnp.float32)
+            back[here, :] = both_back[:, width:]
+            grads.append(both_back[:, :width].astype(jnp.bfloat16))
+            parts.append(part)
+        grad = jnp.concatenate(grads, axis=0)
+        dgates = jnp.concatenate(parts, axis=0)
         holder = lax.div(t, steps)
 
         @pl.when(holder != me_s)
@@ -380,6 +394,7 @@
     )
     sent1[...] = sum1[...].astype(jnp.bfloat16)
     first.start(0)
+    hid_out[...] = hidden[...].reshape(rows, total_steps, hid).astype(jnp.bfloat16)
 
     sum2[...] = jnp.zeros(sum2.shape, jnp.float32)
     gcn_b_sum = jnp.zeros((1, width), jnp.float32)
@@ -504,6 +519,7 @@
         pltpu.VMEM((1, width), f32),
         pltpu.VMEM((1, 4 * hid), f32),
         pltpu.VMEM((rows, total_steps, hid), bf16),
+        pltpu.VMEM((rows * total_steps, hid), f32),
         pltpu.VMEM((rows * total_steps, hid), f32),
         pltpu.VMEM((nv, steps, 8, LANES), jnp.int32),
         pltpu.VMEM((nv, steps, tile, width), bf16),
@@ -538,10 +554,10 @@
     vmem = pl.BlockSpec(memory_space=pltpu.VMEM)
     smem = pl.BlockSpec(memory_space=pltpu.SMEM)
     hbm = pl.BlockSpec(memory_space=pl.ANY)
-    hidden, *grads = pl.pallas_call(
+    results = pl.pallas_call(
         functools.partial(kernel, sizes),
         out_shape=[
-            jax.ShapeDtypeStruct((total_steps, rows, hid), bf16),
+            jax.ShapeDtypeStruct((rows, total_steps, hid), bf16),
             jax.ShapeDtypeStruct((width, width), f32),
             jax.ShapeDtypeStruct((1, width), f32),
             jax.ShapeDtypeStruct((width, 4 * hid), f32),
@@ -566,15 +582,17 @@
         lstm_bias.reshape(1, -1),
         hidden_grad,
     )
-    grad_gcn, grad_gbias, grad_input, grad_recur, grad_bias = pl.pallas_call(
+    count = len(results)
+    hidden, grad_gcn, grad_gbias, grad_input, grad_recur, grad_bias = pl.pallas_call(
         write_out,
-        out_shape=[jax.ShapeDtypeStruct(grad.shape, f32) for grad in grads],
-        in_specs=[hbm] * len(grads),
-        out_specs=[hbm] * len(grads),
-        scratch_shapes=[pltpu.VMEM(grad.shape, f32) for grad in grads] + [dma((2, len(grads)))],
+        out_shape=[jax.ShapeDtypeStruct(each.shape, each.dtype) for each in results],
+        in_specs=[hbm] * count,
+        out_specs=[hbm] * count,
+        scratch_shapes=[pltpu.VMEM(each.shape, each.dtype) for each in results]
+        + [dma((2, count))],
         compiler_params=pltpu.CompilerParams(vmem_limit_bytes=60 * 2**20),
-    )(*grads)
-    hidden_states = jnp.transpose(hidden, (1, 0, 2))[None]
+    )(*results)
+    hidden_states = hidden[None]
     return (
         hidden_states,
         grad_gcn,

time: 64.2 us -> 62.2 us (0.969)
  local copies, waits for them, and re-layouts: 2.18 us -> 0 us
    unnamed x1 -> x0, local copies, waits for them, and re-layouts: 2.18 us -> none
where the time goes in v4:
time: 62.2 us; the launch traced here: 61.8 us
  Pallas kernels  59.8 us (96%)
  other arithmetic  1.37 us (2%)
  between operations  0.64 us (1%)
    pallas_call x1, Pallas kernels, on_device(): pl.pallas_call(functools.partial(kernel, sizes), out_shape=[jax.ShapeDtyp...  57.7 us
    pallas_call x1, Pallas kernels, on_device(): pl.pallas_call(write_out, out_shape=[jax.ShapeDtypeStruct(each.shape, eac...  2.14 us
    select_n x1, other arithmetic, on_device(): places = jnp.where(live, tile_cols // row_blocks, nv)  1.37 us

profile of v4, /device:TPU:0, one launch (start us, length us, event | category | flops | bytes accessed | tf_op | source)
XLA Modules:
  0.0 61.8 jit_solution(17275407474492123506)
XLA Ops:
  0.6 1.4 %fusion.1.place_ref = s32[2,8,8]{2,1,0:T(8,128)} fusion(s32[2,8,8]{2,1,0:T(8,128)} %cols_hbm.1, s32[2,8]{1,0:T(2,128)} %param.13), kind=kLoop, calls=%fused_computation.5 | loop fusion | flops 2176 | bytes 1088 | tf_op jit(solution)/shard_map/jit(_where)/select_n | solution.py:492
  2.0 57.7 %shard_map.145 = (bf16[256,8,128]{2,1,0:T(8,128)(2,1)}, f32[128,128]{1,0:T(8,128)}, f32[1,128]{1,0:T(1,128)}, f32[128,512]{1,0:T(8,128)}, f32[128,512]{1,0:T(8,128)}, /*index=5*/f32[1,512]{1,0:T(1,128)}) custom-call(s32[2,8,8]{2,1,0:T(8,128)} %cols_hbm.1, s32[2,8,8]{2,1,0:T(8,128)} %fusion.1.place_ref, bf16[2,8,128,128]{3,2,1,0:T(8,128)(2,1)} %bitcast.6, ...), custom_call_target="tpu_custom_call" | custom-call | tf_op jit(solution)/shard_map/pallas_call | solution.py:557
  59.7 2.1 %shard_map.146 = (bf16[256,8,128]{2,1,0:T(8,128)(2,1)}, f32[128,128]{1,0:T(8,128)}, f32[1,128]{1,0:T(1,128)}, f32[128,512]{1,0:T(8,128)}, f32[128,512]{1,0:T(8,128)}, /*index=5*/f32[1,512]{1,0:T(1,128)}) custom-call(bf16[256,8,128]{2,1,0:T(8,128)(2,1)} %get-tuple-element.18.refs_0_, f32[128,128]{1,0:T(8,128)} %get-tuple-element.19.refs_1_, ...), custom_call_target="tpu_custom_call" | custom-call | tf_op jit(solution)/shard_map/pallas_call | solution.py:586
